TPU v7x, 128 devices: a whole 4x4x4 slice. The times are simulated.
128 devices in a mesh: req: 8 (over y_lo, x), exp: 16 (over z, y_hi, core).
Axes of the slice: x: 4, y: 4 (y_hi: 2, y_lo: 2; y = y_hi * 2 + y_lo), z: 4, core: 2. Of those that a mesh axis runs over, the one named last changes fastest.
Arguments:
- hidden_in: bfloat16 [2048, 6144], P(('req', 'exp')), may hold values from -6 to 6
- queries: bfloat16 [2048, 6144], P('req', 'exp'), may hold values from -25 to 25
- question_kv: bfloat16 [2048, 2048], P('req'), may hold values from -6 to 6
- passage_kv: bfloat16 [32, 2048, 2048], P('req', 'exp'), may hold values from -25 to 25
- use_lists: int32 [8, 4], replicated, may hold values from 0 to 31, as said below
- offsets: int32 [8, 4], replicated, may hold values from 0 to 6399, as said below
- out_weight: bfloat16 [6144, 6144], P('exp', 'req'), may hold values from -0.078125 to 0.078125
- norm_gain: float32 [6144], replicated, may hold values from 0.1 to 1.9
- router: bfloat16 [6144, 8], replicated, may hold values from -0.078125 to 0.078125
- routes: int32 [2048, 2], P(('req', 'exp')), may hold values from 0 to 7, all different within a row; in each aligned block of 16 rows (0 to 15, 16 to 31, ...) at most 5 rows name the same one
- w_gate: bfloat16 [8, 6144, 8192], P('req', None, 'exp'), may hold values from -0.078125 to 0.078125
- w_up: bfloat16 [8, 6144, 8192], P('req', None, 'exp'), may hold values from -0.078125 to 0.078125
- w_down: bfloat16 [8, 8192, 6144], P('req', 'exp'), may hold values from -0.0625 to 0.0625
Outputs:
- layer_out: bfloat16 [2048, 6144], P(('req', 'exp'))
Inputs may be any that keep to these rules, and one draw needn't show every extreme that they name: `use_lists`: passage p lies with owner p // 4; the 4 passages of one request lie with 4 different owners. `offsets`: slot j starts at j * (2112) plus 0 to 63 positions. `routes`: in the rows of one device no expert is named more than 5 times; the two experts of a row differ.
All inputs are finite; a program needn't handle non-finite values.
Results may differ from a plain program's by a relative error of at most 0.014.
Values may be sent and summed in bfloat16 or wider, within the bound.
A program may use at most 128 MiB of HBM per device.

v0:
```python
import math

import jax
import jax.numpy as jnp
import numpy as np
from jax import lax
from jax.sharding import PartitionSpec as P

D = 6144
HQ = 48
KVH = 8
HD = 128
E = 8
PLEN = 2048
PUSE = 4
GAP = 64
C = 5


ROPE_BASE = 1000000.0
EPSILON = 1e-05


def frequencies():
    half_width = HD // 2
    return ROPE_BASE ** (-(jnp.arange(half_width, dtype=jnp.float32) / half_width))


def rotate(vectors, angles):
    half_width = HD // 2
    cosine = jnp.cos(angles)
    sine_part = jnp.sin(angles)
    lower = vectors[..., :half_width]
    upper = vectors[..., half_width:]
    return jnp.concatenate(
        [lower * cosine - upper * sine_part, upper * cosine + lower * sine_part], axis=-1
    )


def per_device(
    hidden_in,
    queries,
    question_kv,
    passage_kv,
    use_lists,
    offsets,
    out_weight,
    norm_gain,
    router,
    routes,
    w_gate,
    w_up,
    w_down,
):
    req_count = lax.axis_size("req")
    exp_count = lax.axis_size("exp")
    request = lax.axis_index("req")
    member = lax.axis_index("exp")
    q_count = queries.shape[0]
    heads_here = queries.shape[1] // HD
    group_size = HQ // KVH
    pass_here = passage_kv.shape[0]
    block_tok = passage_kv.shape[1]
    head_table = np.array(
        [dest * heads_here // group_size for dest in range(exp_count)], dtype=np.int32
    )
    kv_head = member * heads_here // group_size
    owners = use_lists // pass_here
    local_slot = use_lists % pass_here
    holds = (owners == request)[:, :, None] & (
        local_slot[:, :, None] == jnp.arange(pass_here, dtype=jnp.int32)[None, None, :]
    )
    select_rows = jnp.sum(holds.astype(jnp.float32), axis=1).astype(jnp.bfloat16)
    outgoing = jnp.einsum(
        "rp,pkc->rkc", select_rows, passage_kv, preferred_element_type=jnp.float32
    ).astype(jnp.bfloat16)
    landed = lax.all_to_all(outgoing, "req", split_axis=0, concat_axis=0, tiled=True)
    by_head = landed.reshape(req_count, block_tok, KVH, 2 * HD)[:, :, head_table, :]
    arrived = lax.all_to_all(by_head, "exp", split_axis=2, concat_axis=1, tiled=True).reshape(
        req_count, block_tok * exp_count, 2 * HD
    )
    my_uses = lax.dynamic_index_in_dim(use_lists, request, 0, keepdims=False)
    my_offsets = lax.dynamic_index_in_dim(offsets, request, 0, keepdims=False)
    from_owner = (
        my_uses[:, None] // pass_here == jnp.arange(req_count, dtype=jnp.int32)[None, :]
    ).astype(jnp.bfloat16)
    passages = jnp.einsum(
        "jo,okc->jkc", from_owner, arrived, preferred_element_type=jnp.float32
    ).astype(jnp.bfloat16)
    freq_table = frequencies()
    p_angles = my_offsets.astype(jnp.float32)[:, None, None] * freq_table[None, None, :]
    p_keys = (
        rotate(passages[:, :, :HD].astype(jnp.float32), p_angles)
        .astype(jnp.bfloat16)
        .reshape(-1, HD)
    )
    p_values = passages[:, :, HD:].reshape(-1, HD)
    q_angles = (PUSE * (PLEN + GAP) + jnp.arange(q_count)).astype(jnp.float32)[
        :, None
    ] * freq_table[None, :]
    own_kv = lax.dynamic_slice_in_dim(question_kv, kv_head * 2 * HD, 2 * HD, 1)
    q_keys = rotate(own_kv[:, :HD].astype(jnp.float32), q_angles).astype(jnp.bfloat16)
    all_keys = jnp.concatenate([p_keys, q_keys], axis=0)
    all_values = jnp.concatenate([p_values, own_kv[:, HD:]], axis=0)
    rotated = rotate(
        queries.reshape(q_count, heads_here, HD).astype(jnp.float32), q_angles[:, None, :]
    ).astype(jnp.bfloat16)
    query_rows = rotated.transpose(1, 0, 2).reshape(heads_here * q_count, HD)
    scores = lax.dot_general(
        query_rows, all_keys, (((1,), (1,)), ((), ())), preferred_element_type=jnp.float32
    ) / math.sqrt(HD)
    row_token = jnp.arange(heads_here * q_count) % q_count
    key_token = jnp.arange(all_keys.shape[0]) - PUSE * PLEN
    scores = jnp.where(key_token[None, :] <= row_token[:, None], scores, -jnp.inf)
    highest = jnp.max(scores, axis=-1, keepdims=True)
    weights = jnp.exp(scores - highest)
    probabilities = (weights / jnp.sum(weights, axis=-1, keepdims=True)).astype(jnp.bfloat16)
    attended = jnp.dot(probabilities, all_values, preferred_element_type=jnp.float32).astype(
        jnp.bfloat16
    )
    attended = (
        attended.reshape(heads_here, q_count, HD)
        .transpose(1, 0, 2)
        .reshape(q_count, heads_here * HD)
    )
    head_terms = jnp.dot(
        attended,
        lax.all_gather(out_weight, "req", axis=1, tiled=True),
        preferred_element_type=jnp.float32,
    ).astype(jnp.bfloat16)
    attn_sum = lax.psum_scatter(head_terms, "exp", scatter_dimension=0, tiled=True).astype(
        jnp.float32
    )
    resid = hidden_in.astype(jnp.float32) + attn_sum
    normed = (
        resid * lax.rsqrt(jnp.mean(resid * resid, axis=-1, keepdims=True) + EPSILON) * norm_gain
    ).astype(jnp.bfloat16)
    logits = jnp.dot(normed, router, preferred_element_type=jnp.float32)
    expert_ids = jnp.arange(E, dtype=jnp.int32)
    selected = routes[:, :, None] == expert_ids[None, None, :]
    picked_logits = jnp.sum(jnp.where(selected, logits[:, None, :], 0.0), axis=-1)
    gate_values = jax.nn.sigmoid(picked_logits - picked_logits[:, ::-1])
    tok_here = hidden_in.shape[0]
    flat_routes = routes.reshape(-1)
    one_hot = (flat_routes[:, None] == expert_ids[None, :]).astype(jnp.int32)
    ranks = jnp.sum((jnp.cumsum(one_hot, axis=0) - one_hot) * one_hot, axis=-1)
    slot_ids = flat_routes * C + ranks
    slot_match = jnp.arange(E * C, dtype=jnp.int32)[:, None] == slot_ids[None, :]
    placement = jnp.sum(slot_match.reshape(E * C, tok_here, 2).astype(jnp.float32), axis=-1).astype(
        jnp.bfloat16
    )
    packed = jnp.dot(placement, normed, preferred_element_type=jnp.float32).astype(jnp.bfloat16)
    packed = packed.reshape(req_count, E // req_count, C, D)
    received = lax.all_to_all(packed, "req", split_axis=0, concat_axis=0, tiled=True)
    gathered = lax.all_gather(received, "exp", axis=0, tiled=True)
    token_rows = gathered[:, 0].reshape(-1, D)
    gate_act = jnp.dot(token_rows, w_gate[0], preferred_element_type=jnp.float32)
    up_act = jnp.dot(token_rows, w_up[0], preferred_element_type=jnp.float32)
    inner = (jax.nn.silu(gate_act) * up_act).astype(jnp.bfloat16)
    results = [
        jnp.dot(inner, w_down[0], preferred_element_type=jnp.float32).reshape(
            lax.axis_size("exp") * req_count, C, D
        )
    ]
    summed = lax.psum_scatter(
        jnp.stack(results, axis=1).astype(jnp.bfloat16), "exp", scatter_dimension=0, tiled=True
    )
    returned = lax.all_to_all(summed, "req", split_axis=0, concat_axis=0, tiled=True).reshape(
        E * C, D
    )
    token_match = (
        jnp.arange(E * C, dtype=jnp.int32)[None, None, :]
        == slot_ids.reshape(tok_here, 2)[:, :, None]
    ).astype(jnp.float32)
    gate_matrix = jnp.sum(token_match * gate_values[:, :, None], axis=1)
    mixed = jnp.dot(gate_matrix, returned.astype(jnp.float32), precision=lax.Precision.HIGHEST)
    return (resid + mixed).astype(jnp.bfloat16)


def solution(mesh):
    in_specs = (
        P(("req", "exp"), None),
        P("req", "exp"),
        P("req", None),
        P("req", "exp", None),
        P(),
        P(),
        P("exp", "req"),
        P(),
        P(),
        P(("req", "exp"), None),
        P("req", None, "exp"),
        P("req", None, "exp"),
        P("req", "exp", None),
    )
    out_specs = P(("req", "exp"), None)
    return jax.shard_map(
        per_device, mesh=mesh, in_specs=in_specs, out_specs=out_specs, check_vma=False
    )
```

profile of v0, /device:TPU:1, one launch (start us, length us, event | category | flops | bytes accessed | tf_op | source)
XLA Modules:
  0.0 667.3 jit_solution(9659714269229472276)
XLA Ops:
  6.5 0.8 add_select_fusion.1
  7.4 0.7 fusion.38
  8.1 1.8 convolution_convert_fusion.4
  10.0 4.3 copy.139
  14.2 6.0 all-to-all-start
  20.3 49.6 %all-to-all-done = bf16[8,128,2048]{2,1,0:T(8,128)(2,1)} async-done(((bf16[8,128,2048]{2,1,0:T(8,128)(2,1)}), bf16[8,128,2048]{2,1,0:T(8,128)(2,1)}, u32[]{:S(2)}, u32[]{:S(2)}) %all-to-all-start) | async-done | bytes 4194336 | tf_op jit(solution)/shard_map/all_to_all | solution.py:77
  69.9 6.5 copy.140
  76.4 6.5 copy.141
  82.8 6.9 %gather_fusion = bf16[16,8,128,256]{3,2,1,0:T(8,128)(2,1)} fusion(bf16[8,128,8,256]{3,1,2,0:T(8,128)(2,1)} %copy.141, s32[1024]{0:T(1024)S(1)} %pad_clamp_fusion), kind=kCustom, calls=%fused_computation | custom fusion | bytes 16777280 | tf_op jit(solution)/shard_map/gather | solution.py:78
  89.8 8.6 %all-to-all-start.1 = ((bf16[8,128,16,256]{3,1,0,2:T(8,128)(2,1)}), bf16[8,128,16,256]{3,1,0,2:T(8,128)(2,1)}, u32[]{:S(2)}, u32[]{:S(2)}) async-start(bf16[8,128,16,256]{3,1,0,2:T(8,128)(2,1)} %bitcast.70), calls=%async_computation.1 | async-start | bytes 16777216 | tf_op jit(solution)/shard_map/all_to_all | solution.py:79
  98.5 0.7 all-gather.3.cloned.1.call-update
  99.8 0.9 constant_dynamic-slice_fusion
  100.9 0.3 subtract_convert_fusion.2
  101.8 136.9 %all-to-all-done.1 = bf16[8,128,16,256]{3,1,0,2:T(8,128)(2,1)} async-done(((bf16[8,128,16,256]{3,1,0,2:T(8,128)(2,1)}), bf16[8,128,16,256]{3,1,0,2:T(8,128)(2,1)}, u32[]{:S(2)}, u32[]{:S(2)}) %all-to-all-start.1) | async-done | bytes 8388640 | tf_op jit(solution)/shard_map/all_to_all | solution.py:79
  238.6 12.3 %copy.142 = bf16[8,16,128,1,256]{4,0,2,1,3:T(8,128)(2,1)} copy(bf16[8,16,128,1,256]{4,2,0,1,3:T(8,128)(2,1)} %bitcast.9) | data formatting | bytes 16777216 | tf_op jit(solution)/shard_map/all_to_all | solution.py:79
  251.0 5.8 convolution_convert_fusion.3
  256.7 1.3 slice_convert_fusion
  258.1 4.0 subtract_convert_fusion
  262.1 1.6 copy.146
  263.7 3.5 copy.144
  267.3 1.6 copy.162
  268.9 1.6 copy.143
  270.4 0.6 copy.161
  271.1 12.0 %fusion.1 = (f32[768]{0:T(1024)S(1)}, f32[768,8448]{1,0:T(8,128)}) fusion(s32[8448]{0:T(1024)S(1)} %iota_add_fusion, s32[768]{0:T(1024)S(1)} %add_select_fusion, bf16[768,128]{1,0:T(8,128)(2,1)S(1)} %bitcast.83, bf16[256,64]{0,1:T(8,128)(2,1)S(1)} %get-tuple-element.14, bf16[256,64]{0,1:T(8,128)(2,1)S(1)} %get-tuple-element.13, ...), kind=kOutput, calls=%fused_computation.5 | convolution fusion | flops 1695546624 | bytes 28351488 | tf_op jit(solution)/shard_map/dot_general | solution.py:109
  283.0 11.9 %fusion = f32[768]{0:T(1024)S(1)} fusion(f32[768,8448]{1,0:T(8,128)} %get-tuple-element.20, f32[768]{0:T(1024)S(1)} %get-tuple-element.19, s32[8448]{0:T(1024)S(1)} %iota_add_fusion, s32[768]{0:T(1024)S(1)} %add_select_fusion), kind=kLoop, calls=%fused_computation.4 | loop fusion | flops 32439552 | bytes 25995264 | tf_op jit(solution)/shard_map/reduce_sum | solution.py:117
  295.0 12.0 %fusion.28 = bf16[768,128]{1,0:T(8,128)(2,1)S(1)} fusion(bf16[256,128]{1,0:T(8,128)(2,1)S(1)} %get-tuple-element.10, bf16[8192,128]{1,0:T(8,128)(2,1)S(1)} %bitcast.77, f32[768,8448]{1,0:T(8,128)} %get-tuple-element.20, f32[768]{0:T(1024)S(1)} %fusion, f32[768]{0:T(1024)S(1)} %get-tuple-element.19, s32[8448]{0:T(1024)S(1)} %iota_add_fusion, ...), kind=kOutput, calls=%fused_computation.37 | convolution fusion | flops 1704296448 | bytes 28354560 | tf_op jit(solution)/shard_map/dot_general | solution.py:118
  307.2 5.9 convolution_convert_fusion.1
  313.9 83.2 %reduce-scatter.5.cloned.1.call-done = bf16[16,6144]{1,0:T(8,128)(2,1)} async-done(((bf16[256,6144]{1,0:T(8,128)(2,1)}), bf16[16,6144]{1,0:T(8,128)(2,1)}) %reduce-scatter.5.cloned.1.call-update) | async-done | bytes 196624 | tf_op jit(solution)/shard_map/reduce_scatter | solution.py:131
  397.1 1.1 multiply_reduce_fusion
  398.2 1.3 convolution_convert_fusion.2
  399.5 0.2 reshape.286
  399.7 14.4 %all_to_all.30 = bf16[8,1,5,6144]{3,2,1,0:T(8,128)(2,1)S(1)} all-to-all(bf16[8,1,5,6144]{3,2,1,0:T(8,128)(2,1)S(1)} %bitcast.76), channel_id=1, replica_groups=mesh['req'=8,'exp'=16] {'req'}, dimensions={0} | all-to-all | bytes 983040 | tf_op jit(solution)/shard_map/all_to_all | solution.py:154
  414.1 1.1 copy.152
  415.3 71.9 %all-gather.5.cloned.1.call-done = bf16[128,1,5,6144]{3,0,2,1:T(8,128)(2,1)} async-done(((bf16[8,1,5,6144]{3,0,2,1:T(8,128)(2,1)}), bf16[128,1,5,6144]{3,0,2,1:T(8,128)(2,1)}) %all-gather.5.cloned.1.call-update) | async-done | bytes 7864336 | tf_op jit(solution)/shard_map/all_gather | solution.py:155
  487.1 12.0 %copy.153 = bf16[128,1,5,6144]{3,2,0,1:T(8,128)(2,1)} copy(bf16[128,1,5,6144]{3,0,2,1:T(8,128)(2,1)} %all-gather.5.cloned.1.call-done) | data formatting | bytes 15728640 | tf_op jit(solution)/shard_map/all_gather | solution.py:155
  499.1 14.1 %reshape_squeeze.3 = bf16[640,6144]{1,0:T(8,128)(2,1)} reshape(bf16[128,1,5,6144]{3,2,0,1:T(8,128)(2,1)} %copy.153) | data formatting | bytes 15728640 | tf_op jit(solution)/shard_map/reshape;squeeze | solution.py:156
  513.1 8.5 %fusion.8 = f32[640,512]{1,0:T(8,128)S(1)} fusion(bf16[640,6144]{1,0:T(8,128)(2,1)} %reshape_squeeze.3, bf16[1,6144,512]{2,1,0:T(8,128)(2,1)} %param.25), kind=kOutput, calls=%fused_computation.16 | convolution fusion | flops 4026531840 | bytes 15466496 | tf_op jit(solution)/shard_map/dot_general | solution.py:157
  521.7 7.2 %fusion.25 = bf16[640,512]{1,0:T(8,128)(2,1)S(1)} fusion(bf16[640,6144]{1,0:T(8,128)(2,1)S(1)} %copy-done.3, bf16[1,6144,512]{2,1,0:T(8,128)(2,1)} %param.26, f32[640,512]{1,0:T(8,128)S(1)} %fusion.8), kind=kOutput, calls=%fused_computation.36 | convolution fusion | flops 4028497920 | bytes 16121856 | tf_op jit(solution)/shard_map/dot_general | solution.py:158
  528.8 0.3 dot_general.44
  529.1 9.2 %fusion.50 = bf16[16,8,5,6144]{3,1,0,2:T(8,128)(2,1)} fusion(bf16[1,512,6144]{2,1,0:T(8,128)(2,1)} %param.27, bf16[128,5,512]{2,1,0:T(8,128)(2,1)S(1)} %dot_general.44), kind=kOutput, calls=%fused_computation.103 | convolution fusion | flops 4030464000 | bytes 14811136 | tf_op jit(solution)/shard_map/dot_general | solution.py:161
  538.4 7.3 %copy.163 = bf16[16,8,5,6144]{3,1,2,0:T(8,128)(2,1)} copy(bf16[16,8,5,6144]{3,1,0,2:T(8,128)(2,1)} %fusion.50) | data formatting | bytes 15728640
  545.6 0.9 copy-done.6
  546.6 0.2 fusion.49
  546.9 91.9 %reduce-scatter.7.cloned.1.call-done = bf16[8,30720]{1,0:T(8,128)(2,1)} async-done(((bf16[128,30720]{1,0:T(8,128)(2,1)}), bf16[8,30720]{1,0:T(8,128)(2,1)}) %reduce-scatter.7.cloned.1.call-update) | async-done | bytes 491536
  638.7 2.2 copy.155
  640.9 4.2 all-to-all-start.3
  645.3 12.8 %all-to-all-done.3 = bf16[8,1,5,6144]{3,2,1,0:T(8,128)(2,1)S(1)} async-done(((bf16[8,1,5,6144]{3,2,1,0:T(8,128)(2,1)}), bf16[8,1,5,6144]{3,2,1,0:T(8,128)(2,1)S(1)}, u32[]{:S(2)}, u32[]{:S(2)}) %all-to-all-start.3) | async-done | bytes 491552 | tf_op jit(solution)/shard_map/all_to_all | solution.py:168
  658.3 2.1 fusion.4
  (68 shorter events, 2.9 us)
Async XLA Ops:
  6.5 1.6 copy-start
  14.2 6.0 copy-start.12
  14.2 55.6 %all-to-all-start = ((bf16[8,128,2048]{2,1,0:T(8,128)(2,1)}), bf16[8,128,2048]{2,1,0:T(8,128)(2,1)}, u32[]{:S(2)}, u32[]{:S(2)}) async-start(bf16[8,128,2048]{2,1,0:T(8,128)(2,1)} %copy.139), calls=%async_computation | async-start | bytes 8388608 | tf_op jit(solution)/shard_map/all_to_all | solution.py:77
  89.8 9.6 %copy-start.9 = (s32[8,4]{0,1:T(4,128)S(1)}, s32[8,4]{0,1:T(4,128)}, u32[]{:S(2)}) copy-start(s32[8,4]{0,1:T(4,128)} %param.19) | copy-start | bytes 388
  89.8 9.8 %copy-start.7 = (bf16[256,384]{1,0:T(8,128)(2,1)S(1)}, bf16[256,384]{1,0:T(8,128)(2,1)}, u32[]{:S(2)}) copy-start(bf16[256,384]{1,0:T(8,128)(2,1)} %param.16) | copy-start | bytes 589828
  89.8 11.6 %copy-start.11 = (s32[8,4]{0,1:T(4,128)S(1)}, s32[8,4]{0,1:T(4,128)}, u32[]{:S(2)}) copy-start(s32[8,4]{0,1:T(4,128)} %param.20) | copy-start | bytes 388
  89.8 148.8 %all-to-all-start.1 = ((bf16[8,128,16,256]{3,1,0,2:T(8,128)(2,1)}), bf16[8,128,16,256]{3,1,0,2:T(8,128)(2,1)}, u32[]{:S(2)}, u32[]{:S(2)}) async-start(bf16[8,128,16,256]{3,1,0,2:T(8,128)(2,1)} %bitcast.70), calls=%async_computation.1 | async-start | bytes 16777216 | tf_op jit(solution)/shard_map/all_to_all | solution.py:79
  98.4 208.8 %all-gather.3.cloned.1.call-start = ((), (), s32[]{:S(2)}) async-start(), calls=%async_computation.6 | async-start | bytes 5308416 | tf_op jit(solution)/shard_map/all_gather | solution.py:128
  99.2 297.9 %reduce-scatter.5.cloned.1.call-start = ((), (), s32[]{:S(2)}) async-start(), calls=%async_computation.7 | async-start | bytes 3342336 | tf_op jit(solution)/shard_map/reduce_scatter | solution.py:131
  263.7 5.2 copy-start.2
  283.0 11.9 %copy-start.4 = (bf16[4,2048,128]{2,1,0:T(8,128)(2,1)S(1)}, bf16[4,2048,128]{2,1,0:T(8,128)(2,1)}, u32[]{:S(2)}) copy-start(bf16[4,2048,128]{2,1,0:T(8,128)(2,1)} %copy.146) | copy-start | bytes 6291460
  307.2 6.0 copy-start.10
  307.2 89.9 %copy-start.5 = (bf16[16,6144]{1,0:T(8,128)(2,1)S(1)}, bf16[16,6144]{1,0:T(8,128)(2,1)}, u32[]{:S(2)}) copy-start(bf16[16,6144]{1,0:T(8,128)(2,1)} %param.15) | copy-start | bytes 589828
  307.2 91.0 %copy-start.8 = (f32[6144]{0:T(1024)S(1)}, f32[6144]{0:T(1024)}, u32[]{:S(2)}) copy-start(f32[6144]{0:T(1024)} %param.22) | copy-start | bytes 73732
  313.1 174.0 %all-gather.5.cloned.1.call-start = ((), (), s32[]{:S(2)}) async-start(), calls=%async_computation.8 | async-start | bytes 8355840 | tf_op jit(solution)/shard_map/all_gather | solution.py:155
  415.2 223.5 %reduce-scatter.7.cloned.1.call-start = ((), (), s32[]{:S(2)}) async-start(), calls=%async_computation.9 | async-start | bytes 8355840
  513.1 8.5 %copy-start.3 = (bf16[640,6144]{1,0:T(8,128)(2,1)S(1)}, bf16[640,6144]{1,0:T(8,128)(2,1)}, u32[]{:S(2)}) copy-start(bf16[640,6144]{1,0:T(8,128)(2,1)} %reshape_squeeze.3) | copy-start | bytes 23592964
  545.6 0.9 copy-start.6
  545.6 1.0 copy-start.13
  546.6 113.7 %copy-start.1 = (bf16[4,128,2048]{2,1,0:T(8,128)(2,1)S(1)}, bf16[4,128,2048]{2,1,0:T(8,128)(2,1)}, u32[]{:S(2)}) copy-start(bf16[4,128,2048]{2,1,0:T(8,128)(2,1)} %param.18) | copy-start | bytes 6291460
  640.9 17.1 %all-to-all-start.3 = ((bf16[8,1,5,6144]{3,2,1,0:T(8,128)(2,1)}), bf16[8,1,5,6144]{3,2,1,0:T(8,128)(2,1)S(1)}, u32[]{:S(2)}, u32[]{:S(2)}) async-start(bf16[8,1,5,6144]{3,2,1,0:T(8,128)(2,1)} %copy.155), calls=%async_computation.4 | async-start | bytes 1572864 | tf_op jit(solution)/shard_map/all_to_all | solution.py:168
Sparse Core Ops, SparseCore 0:
  100.9 70.3 all-gather.2
  313.2 83.8 reduce-scatter.4
  415.3 71.7 all-gather.4
  545.8 92.9 reduce-scatter.6
where the time goes:
time: 673 us; the launch traced here: 667 us
  waiting for transfers between devices  447 us (66%)
  local copies, waits for them, and re-layouts  85.8 us (13%)
  matrix products  65.9 us (10%)
  other arithmetic  21.3 us (3%)
  starting transfers between devices  19.2 us (3%)
  blocking collectives  14.4 us (2%)
  between operations  13.9 us (2%)
    all_to_all x1, waiting for transfers between devices, per_device(): lax.all_to_all(by_head, 'exp', split_axis=2, concat_axis=1, tiled=True)  137 us
    unnamed x5, waiting for transfers between devices  92.6 us
    reduce_scatter x1, waiting for transfers between devices, per_device(): lax.psum_scatter(head_terms, 'exp', scatter_dimension=0, tiled=True)  83.2 us
    all_gather x1, waiting for transfers between devices, per_device(): gathered = lax.all_gather(received, 'exp', axis=0, tiled=True)  71.9 us
    all_to_all x1, waiting for transfers between devices, per_device(): lax.all_to_all(outgoing, 'req', split_axis=0, concat_axis=0, tiled=True)  49.6 us
    all_to_all x1, blocking collectives, per_device(): lax.all_to_all(packed, 'req', split_axis=0, concat_axis=0, tiled=True)  14.4 us
    another operation x1, local copies, waits for them, and re-layouts, per_device(): token_rows = gathered[:, 0].reshape(-1, D)  14.1 us
  transfers between devices with their start and end apart: 7, of which 6 were waited for; matrix products, arithmetic and copies ran while one was open for 11% of the time, Pallas kernels for 0%

commit v1 on v0

v1 whole, which is shorter than its diff:
```python
import math

import jax
import jax.numpy as jnp
import numpy as np
from jax import lax
from jax.experimental import pallas as pl
from jax.experimental.pallas import tpu as pltpu
from jax.sharding import PartitionSpec as P

D = 6144
HALF = D // 2
HQ = 48
KVH = 8
HD = 128
E = 8
PLEN = 2048
PUSE = 4
PASS_DEV = 4
GAP = 64
C = 5
QTOK = 256
TOK = 16
N_REQ = 8
HID = 512
COLS = D // N_REQ
HEADS = 3
ROPE_BASE = 1000000.0
EPSILON = 1e-05
MESH = pl.DeviceIdType.MESH
F32 = jnp.float32
BF16 = jnp.bfloat16
VMEM = pl.BlockSpec(memory_space=pltpu.VMEM)
SMEM = pl.BlockSpec(memory_space=pltpu.SMEM)
ANY = pl.BlockSpec(memory_space=pl.ANY)
SCALE2 = math.log2(math.e) / math.sqrt(HD)
CHUNKS = (0, 1, 3, 2)


def place():
    req = lax.axis_index("req")
    exp = lax.axis_index("exp")
    return req, exp, exp // 4, (exp // 2) % 2, exp % 2


def member(z, yh, c):
    return (z * 2 + yh) * 2 + c


def remote(src, dst, send, recv, device):
    return pltpu.make_async_remote_copy(
        src_ref=src, dst_ref=dst, send_sem=send, recv_sem=recv, device_id=device, device_id_type=MESH
    )


def greet(devices):
    barrier = pltpu.get_barrier_semaphore()
    for device in devices:
        pl.semaphore_signal(barrier, inc=1, device_id=device, device_id_type=MESH)
    pl.semaphore_wait(barrier, len(devices))


def turn(vectors, cosine, sine):
    return vectors * cosine + pltpu.roll(vectors, HD // 2, vectors.ndim - 1) * sine


def attention_kernel(
    pkv, q_in, qkv, sel, own, pcos, psin, qcos, qsin, out,
    land0, land1, land2, land3, stage, got0, got1, got2, got3,
    kown, ksib, qrot, kvq, acc, top, low,
    s1s, s1r, s2s, s2r, fs, fr, ls,
):
    req, exp, z, yh, c = place()
    mine = req * 2 + yh
    land = (land0, land1, land2, land3)
    got = (got0, got1, got2, got3)
    sibling = (req, member(z, yh, 1 - c))
    head = exp // 2
    load_q = pltpu.make_async_copy(qkv.at[:, pl.ds(pl.multiple_of(head * 256, 256), 256)], kvq, ls)
    load_q.start()

    devices = [(req, member((z + d) % 4, yh, c)) for d in range(1, 4)] + [sibling]
    for k in range(1, 16):
        there = (mine + k) % 16
        devices.append((there // 2, member(z, there % 2, c)))
    greet(devices)

    def cols(zt):
        return pl.ds(pl.multiple_of(zt * 512, 512), 512)

    firsts = []
    for d in range(1, 4):
        zt = (z + d) % 4
        cp = remote(
            pkv.at[:, :, cols(zt)], land[4 - d], s1s.at[d], s1r.at[4 - d],
            (req, member(zt, yh, c)),
        )
        cp.start()
        firsts.append(cp)
    local = pltpu.make_async_copy(pkv.at[:, :, cols(z)], land0, s1r.at[0])
    local.start()

    def half(yt):
        return pl.ds(pl.multiple_of(yt * 256, 256), 256)

    def second(i, k):
        there = (mine + k) % 16
        return remote(
            stage.at[i, there // 2, :, half(there % 2)], got[i].at[mine],
            s2s.at[i, k], s2r.at[i, mine], (there // 2, member(z, there % 2, c)),
        )

    def second_in(i, k):
        there = (mine + k) % 16
        return remote(
            stage.at[i, there // 2, :, half(there % 2)], got[i].at[there],
            s2s.at[i, k], s2r.at[i, there], (there // 2, member(z, there % 2, c)),
        )

    def second_local(i):
        return pltpu.make_async_copy(
            stage.at[i, req, :, half(yh)], got[i].at[mine], s2r.at[i, mine]
        )

    def loop(count, body):
        lax.fori_loop(0, count, lambda k, carry: (body(k), carry)[1], 0)

    for i, d in enumerate(CHUNKS):
        if d == 0:
            local.wait()
        else:
            firsts[(4 - d) - 1].wait_recv()
        for r in range(N_REQ):
            stage[i, r] = land[d][sel[r]]
        loop(15, lambda k: second(i, k + 1).start())
        second_local(i).start()

        if i == 0:
            load_q.wait()
            cosine, sine = qcos[...], qsin[...]
            for h in range(HEADS):
                qrot[h] = turn(q_in[:, h * HD : (h + 1) * HD].astype(F32), cosine, sine).astype(BF16)
            keys = turn(kvq[:, :HD].astype(F32), cosine, sine).astype(BF16)
            values = kvq[:, HD:]
            row = lax.broadcasted_iota(jnp.int32, (QTOK, QTOK), 0)
            col = lax.broadcasted_iota(jnp.int32, (QTOK, QTOK), 1)
            for h in range(HEADS):
                s = lax.dot_general(
                    qrot[h], keys, (((1,), (1,)), ((), ())), preferred_element_type=F32
                )
                s = jnp.where(col <= row, s, -jnp.inf)
                t = jnp.max(s, axis=-1, keepdims=True)
                p = jnp.exp2(s * SCALE2 - t * SCALE2)
                top[h] = jnp.broadcast_to(t, (QTOK, HD))
                low[h] = jnp.broadcast_to(jnp.sum(p, axis=-1, keepdims=True), (QTOK, HD))
                acc[h] = jnp.dot(p.astype(BF16), values, preferred_element_type=F32)

    def attend(block):
        def one(h):
            s = lax.dot_general(
                qrot[h], block[:, :HD], (((1,), (1,)), ((), ())), preferred_element_type=F32
            )
            before = top[h][:, :1]
            t = jnp.maximum(before, jnp.max(s, axis=-1, keepdims=True))
            p = jnp.exp2(s * SCALE2 - t * SCALE2)
            alpha = jnp.exp2((before - t) * SCALE2)
            top[h] = jnp.broadcast_to(t, (QTOK, HD))
            low[h] = low[h] * alpha + jnp.sum(p, axis=-1, keepdims=True)
            acc[h] = acc[h] * alpha + jnp.dot(
                p.astype(BF16), block[:, HD:], preferred_element_type=F32
            )

        loop(HEADS, one)

    passes = []
    for i in range(4):
        loop(15, lambda k: second_in(i, k + 1).wait_recv())
        second_local(i).wait()
        for j in range(PUSE):
            cosine, sine = pcos[pl.ds(j, 1), :], psin[pl.ds(j, 1), :]
            for y in range(2):
                kv = got[i][own[j] * 2 + y]
                rows = pl.ds(j * 256 + y * 128, 128)
                kown[i, rows, :HD] = turn(kv[:, :HD].astype(F32), cosine, sine).astype(BF16)
                kown[i, rows, HD:] = kv[:, HD:]
        cp = remote(kown.at[i], ksib.at[i], fs.at[i], fr.at[i], sibling)
        cp.start()
        passes.append(cp)
        attend(kown.at[i])
        cp.wait_recv()
        attend(ksib.at[i])

    for h in range(HEADS):
        out[:, h * HD : (h + 1) * HD] = (acc[h] / low[h]).astype(BF16)
    for cp in firsts:
        cp.wait_send()
    for i in range(4):
        loop(15, lambda k: second(i, k + 1).wait_send())
        passes[i].wait_send()


def attention(passage_kv, queries, question_kv, sel, own, pcos, psin, qcos, qsin):
    dma = pltpu.SemaphoreType.DMA
    return pl.pallas_call(
        attention_kernel,
        out_shape=jax.ShapeDtypeStruct((QTOK, HEADS * HD), BF16),
        in_specs=[ANY, VMEM, ANY, SMEM, SMEM, VMEM, VMEM, VMEM, VMEM],
        out_specs=VMEM,
        scratch_shapes=[pltpu.VMEM((PASS_DEV, 128, 512), BF16)] * 4
        + [pltpu.VMEM((4, N_REQ, 128, 512), BF16)]
        + [pltpu.VMEM((16, 128, 256), BF16)] * 4
        + [
            pltpu.VMEM((4, 1024, 256), BF16),
            pltpu.VMEM((4, 1024, 256), BF16),
            pltpu.VMEM((HEADS, QTOK, HD), BF16),
            pltpu.VMEM((QTOK, 256), BF16),
            pltpu.VMEM((HEADS, QTOK, HD), F32),
            pltpu.VMEM((HEADS, QTOK, HD), F32),
            pltpu.VMEM((HEADS, QTOK, HD), F32),
            dma((4,)), dma((4,)), dma((4, 16)), dma((4, 16)), dma((4,)), dma((4,)), dma,
        ],
        name="attend_passages",
        compiler_params=pltpu.CompilerParams(
            collective_id=0, has_side_effects=True, vmem_limit_bytes=48 << 20
        ),
    )(passage_kv, queries, question_kv, sel, own, pcos, psin, qcos, qsin)


def project_kernel(
    att, w, hid, gain, router, spots, diff, first, second, resid_out, packed_out, gates_out,
    attb, ownp, sibs, sibr, rss, rsr, fsend, fin, nsend, nbuf, pbuf, gbuf,
    a_s, a_r, b_s, b_r, c_s, c_r, d_s, d_r, e_s, e_r,
):
    req, exp, z, yh, c = place()
    chip = exp // 2
    sibling = (req, member(z, yh, 1 - c))
    peers = [((req + d) % N_REQ, exp) for d in range(1, 8)]
    chips = [(req, ((chip + d) % 8) * 2 + c) for d in range(1, 8)]
    greet(peers + chips + [sibling])

    sends = []
    for d in range(7, 0, -1):
        cp = remote(att, attb.at[8 - d], a_s.at[d], a_r.at[8 - d], peers[d - 1])
        cp.start()
        sends.append(cp)
    by_turn = {8 - d: cp for d, cp in zip(range(7, 0, -1), sends)}

    def multiply(k):
        source = att if k == 0 else attb.at[k]
        if k > 0:
            by_turn[k].wait_recv()
        theirs = source[:, 1 - c].reshape(128, 384)
        sibs[k] = jnp.dot(theirs, w[...], preferred_element_type=F32).astype(BF16).reshape(8, TOK, COLS)
        cp = remote(sibs.at[k], sibr.at[k], b_s.at[k], b_r.at[k], sibling)
        cp.start()
        ours = source[:, c].reshape(128, 384)
        ownp[k] = jnp.dot(ours, w[...], preferred_element_type=F32).reshape(8, TOK, COLS)
        return cp

    def scatter(k, cp):
        cp.wait_recv()
        rss[k] = (ownp[k] + sibr[k].astype(F32)).astype(BF16)
        rsr[k, chip] = rss[k, chip]
        copies = []
        for d in range(1, 8):
            there = (chip + d) % 8
            cp = remote(rss.at[k, there], rsr.at[k, chip], c_s.at[k, d], c_r.at[k, d], chips[d - 1])
            cp.start()
            copies.append(cp)
        return copies

    def finish(k, copies):
        for cp in copies:
            cp.wait_recv()
        total = jnp.sum(rsr[k].astype(F32), axis=0).astype(BF16)
        if k == 0:
            fin[req] = total
            return None
        fsend[k] = total
        cp = remote(fsend.at[k], fin.at[req], d_s.at[k], d_r.at[k], peers[k - 1])
        cp.start()
        return cp

    halves, parts, ends = {}, {}, {}
    for k in range(8 + 4):
        if k < 8:
            halves[k] = multiply(k)
        if 0 <= k - 1 < 8:
            parts[k - 1] = scatter(k - 1, halves[k - 1])
        if 0 <= k - 4 < 8:
            ends[k - 4] = finish(k - 4, parts[k - 4])
    for k in range(1, 8):
        ends[k].wait_recv()

    attn = jnp.concatenate([fin[i] for i in range(N_REQ)], axis=1).astype(F32)
    resid = hid[...].astype(F32) + attn
    resid_out[...] = resid
    mean = jnp.mean(resid * resid, axis=-1, keepdims=True)
    normed = (resid * lax.rsqrt(mean + EPSILON) * gain[...]).astype(BF16)

    left, right = normed[:, :HALF], normed[:, HALF:]
    nsend[...] = jnp.where(c == 0, right, left)
    nbuf[c] = jnp.where(c == 0, left, right)
    pbuf[c] = spots[...]
    lasts = [
        remote(nsend, nbuf.at[c], e_s.at[0], e_r.at[0], sibling),
        remote(spots, pbuf.at[c], e_s.at[1], e_r.at[1], sibling),
    ]
    for cp in lasts:
        cp.start()
    logits = jnp.dot(normed, router[...], preferred_element_type=F32)
    apart = jnp.sum(logits * diff[...], axis=-1, keepdims=True)
    gates = first[...] * jax.nn.sigmoid(apart) + second[...] * jax.nn.sigmoid(-apart)
    gbuf[c] = gates
    cp = remote(gbuf.at[c], gbuf.at[c], e_s.at[2], e_r.at[2], sibling)
    cp.start()
    lasts.append(cp)
    lasts[0].wait_recv()
    lasts[1].wait_recv()
    packed_out[...] = (
        lax.dot_general(
            pbuf[...].reshape(32, 128), nbuf[...].reshape(32, HALF), (((0,), (0,)), ((), ())),
            preferred_element_type=F32,
        )
        .astype(BF16)
        .reshape(E, TOK, HALF)
    )
    lasts[2].wait_recv()
    gates_out[...] = gbuf[...]

    for cp in sends + lasts:
        cp.wait_send()
    for k in range(8):
        halves[k].wait_send()
        for cp in parts[k]:
            cp.wait_send()
        if k > 0:
            ends[k].wait_send()


def project(att, w, hid, gain, router, spots, diff, first, second):
    dma = pltpu.SemaphoreType.DMA
    v = pltpu.VMEM
    return pl.pallas_call(
        project_kernel,
        out_shape=(
            jax.ShapeDtypeStruct((TOK, D), F32),
            jax.ShapeDtypeStruct((E, TOK, HALF), BF16),
            jax.ShapeDtypeStruct((2, TOK, 128), F32),
        ),
        in_specs=[VMEM] * 9,
        out_specs=(VMEM,) * 3,
        scratch_shapes=[
            v((8, 8, 2, TOK, 384), BF16),
            v((8, 8, TOK, COLS), F32),
            v((8, 8, TOK, COLS), BF16),
            v((8, 8, TOK, COLS), BF16),
            v((8, 8, TOK, COLS), BF16),
            v((8, 8, TOK, COLS), BF16),
            v((8, TOK, COLS), BF16),
            v((8, TOK, COLS), BF16),
            v((TOK, HALF), BF16),
            v((2, TOK, HALF), BF16),
            v((2, TOK, 128), BF16),
            v((2, TOK, 128), F32),
            dma((8,)), dma((8,)), dma((8,)), dma((8,)), dma((8, 8)), dma((8, 8)),
            dma((8,)), dma((8,)), dma((3,)), dma((3,)),
        ],
        name="project_heads",
        compiler_params=pltpu.CompilerParams(
            collective_id=1, has_side_effects=True, vmem_limit_bytes=48 << 20
        ),
    )(att, w, hid, gain, router, spots, diff, first, second)


def expert_kernel(
    packed, gates, resid, pick, spread, wg_h, wu_h, wd_h, out,
    wg, wu, wd, prx, xo, xs, inner, po, sps, spr, rzs, rz, ysend, ry, bsend, ret, msend, mrecv,
    w_s, a_s, a_r, y_s, y_r, g_s, g_r, f_s, f_r, p_s, p_r, r_s, r_r, t_s, t_r, m_s, m_r,
):
    req, exp, z, yh, c = place()
    other = 1 - yh
    sibling = (req, member(z, yh, 1 - c))
    across = (req, member(z, other, c))
    up = (req, member((z + 1) % 4, yh, c))
    down = (req, member((z + 3) % 4, yh, c))
    peers = [((req + d) % N_REQ, exp) for d in range(1, 8)]
    loads = [
        pltpu.make_async_copy(src, dst, w_s.at[i])
        for i, (src, dst) in enumerate(((wg_h, wg), (wu_h, wu), (wd_h, wd)))
    ]
    for cp in loads:
        cp.start()
    greet(peers + [sibling, across, up, down])

    started = []

    def go(cp):
        cp.start()
        started.append(cp)
        return cp

    arrive = []
    for d in range(1, 8):
        there = (req + d) % N_REQ
        arrive.append(
            go(remote(packed.at[there], prx.at[req], a_s.at[d], a_r.at[d], peers[d - 1]))
        )
    prx[req] = packed[req]
    for cp in arrive:
        cp.wait_recv()
    xo[0, yh] = jnp.dot(
        pick[...], prx[...].reshape(128, HALF), preferred_element_type=F32
    ).astype(BF16)

    def share(i, zr, y):
        return go(remote(xo.at[zr, y], xs.at[zr, y], f_s.at[i], f_r.at[i], sibling))

    own_y = go(remote(xo.at[0, yh], xo.at[0, yh], y_s.at[0], y_r.at[0], across))
    up1 = go(remote(xo.at[0, yh], xo.at[3, yh], g_s.at[0], g_r.at[0], up))
    down1 = go(remote(xo.at[0, yh], xo.at[1, yh], g_s.at[1], g_r.at[1], down))
    shares = {}
    shares[0, 0] = share(0, 0, yh)
    own_y.wait_recv()
    up2 = go(remote(xo.at[0, other], xo.at[3, other], g_s.at[2], g_r.at[2], up))
    down2 = go(remote(xo.at[0, other], xo.at[1, other], g_s.at[3], g_r.at[3], down))
    shares[0, 1] = share(1, 0, other)
    up1.wait_recv()
    up3 = go(remote(xo.at[3, yh], xo.at[2, yh], g_s.at[4], g_r.at[4], up))
    shares[3, 0] = share(2, 3, yh)
    down1.wait_recv()
    shares[1, 0] = share(3, 1, yh)

    def hidden(zr):
        shares[zr, 0].wait_recv()
        shares[zr, 1].wait_recv()
        a, b = xo.at[zr], xs.at[zr]
        mine = pl.ds(pl.multiple_of(c * HALF, HALF), HALF)
        theirs = pl.ds(pl.multiple_of((1 - c) * HALF, HALF), HALF)

        def tile(n, carry):
            cols = pl.ds(pl.multiple_of(n * 256, 256), 256)
            x, y = a[...].reshape(160, HALF), b[...].reshape(160, HALF)
            g = jnp.dot(x, wg[mine, cols], preferred_element_type=F32)
            g = g + jnp.dot(y, wg[theirs, cols], preferred_element_type=F32)
            u = jnp.dot(x, wu[mine, cols], preferred_element_type=F32)
            u = u + jnp.dot(y, wu[theirs, cols], preferred_element_type=F32)
            inner[zr, :, cols] = (jax.nn.silu(g) * u).astype(BF16)
            return carry

        lax.fori_loop(0, 2, tile, 0)

    def result(zr):
        def tile(n, carry):
            cols = pl.ds(pl.multiple_of(n * 512, 512), 512)
            theirs = pl.ds(pl.multiple_of((1 - c) * HALF + n * 512, 512), 512)
            mine = pl.ds(pl.multiple_of(c * HALF + n * 512, 512), 512)
            sps[zr, :, :, cols] = (
                jnp.dot(inner[zr], wd[:, theirs], preferred_element_type=F32)
                .astype(BF16)
                .reshape(2, 80, 512)
            )
            po[zr, :, :, cols] = jnp.dot(
                inner[zr], wd[:, mine], preferred_element_type=F32
            ).reshape(2, 80, 512)
            return carry

        lax.fori_loop(0, 6, tile, 0)
        return go(remote(sps.at[zr], spr.at[zr], p_s.at[zr], p_r.at[zr], sibling))

    loads[0].wait()
    loads[1].wait()
    hidden(0)
    down2.wait_recv()
    down3 = go(remote(xo.at[1, other], xo.at[2, other], g_s.at[5], g_r.at[5], down))
    shares[1, 1] = share(4, 1, other)
    up2.wait_recv()
    shares[3, 1] = share(5, 3, other)
    loads[2].wait()
    hidden(1)
    sums = {}
    sums[1] = result(1)
    hidden(3)
    sums[3] = result(3)
    sums[0] = result(0)

    def total(zr, y):
        return po[zr, y] + spr[zr, y].astype(F32)

    sums[1].wait_recv()
    rzs[0] = total(1, other).astype(BF16)
    to_up = go(remote(rzs.at[0], rz.at[0], r_s.at[0], r_r.at[0], up))
    sums[3].wait_recv()
    rzs[1] = total(3, yh).astype(BF16)
    to_down = go(remote(rzs.at[1], rz.at[1], r_s.at[1], r_r.at[1], down))
    up3.wait_recv()
    shares[2, 0] = share(6, 2, yh)
    down3.wait_recv()
    shares[2, 1] = share(7, 2, other)
    hidden(2)
    sums[2] = result(2)
    sums[2].wait_recv()
    rzs[2] = total(2, yh).astype(BF16)
    far_up = go(remote(rzs.at[2], rz.at[2], r_s.at[2], r_r.at[2], up))
    rzs[3] = total(2, other).astype(BF16)
    far_down = go(remote(rzs.at[3], rz.at[3], r_s.at[3], r_r.at[3], down))
    far_up.wait_recv()
    rzs[4] = (total(1, yh) + rz[2].astype(F32)).astype(BF16)
    near_up = go(remote(rzs.at[4], rz.at[4], r_s.at[4], r_r.at[4], up))
    far_down.wait_recv()
    rzs[5] = (total(3, other) + rz[3].astype(F32)).astype(BF16)
    near_down = go(remote(rzs.at[5], rz.at[5], r_s.at[5], r_r.at[5], down))
    sums[0].wait_recv()
    to_up.wait_recv()
    near_down.wait_recv()
    ysend[...] = (
        total(0, other) + rz[0].astype(F32) + rz[5].astype(F32)
    ).astype(BF16)
    cross = go(remote(ysend, ry, y_s.at[1], y_r.at[1], across))
    to_down.wait_recv()
    near_up.wait_recv()
    kept = total(0, yh) + rz[1].astype(F32) + rz[4].astype(F32)
    cross.wait_recv()
    done = (kept + ry[...].astype(F32)).astype(BF16)
    bsend[...] = (
        jnp.dot(spread[...], done, preferred_element_type=F32).astype(BF16).reshape(N_REQ, TOK, HALF)
    )
    back = []
    for d in range(1, 8):
        there = (req + d) % N_REQ
        back.append(
            go(remote(bsend.at[there], ret.at[req], t_s.at[d], t_r.at[d], peers[d - 1]))
        )
    ret[req] = bsend[req]
    for cp in back:
        cp.wait_recv()
    rows = ret[...].reshape(128, HALF).astype(F32)
    msend[...] = jnp.dot(
        gates[1 - c], rows, precision=lax.Precision.HIGHEST, preferred_element_type=F32
    )
    mix = go(remote(msend, mrecv, m_s, m_r, sibling))
    ours = jnp.dot(gates[c], rows, precision=lax.Precision.HIGHEST, preferred_element_type=F32)
    mine = pl.ds(pl.multiple_of(c * HALF, HALF), HALF)
    theirs = pl.ds(pl.multiple_of((1 - c) * HALF, HALF), HALF)
    out[:, mine] = (resid[:, mine] + ours).astype(BF16)
    mix.wait_recv()
    out[:, theirs] = (resid[:, theirs] + mrecv[...]).astype(BF16)
    for cp in started:
        cp.wait_send()


def experts(packed, gates, resid, pick, spread, wg, wu, wd):
    dma = pltpu.SemaphoreType.DMA
    v = pltpu.VMEM
    return pl.pallas_call(
        expert_kernel,
        out_shape=jax.ShapeDtypeStruct((TOK, D), BF16),
        in_specs=[VMEM] * 5 + [ANY] * 3,
        out_specs=VMEM,
        scratch_shapes=[
            v((D, HID), BF16), v((D, HID), BF16), v((HID, D), BF16),
            v((N_REQ, TOK, HALF), BF16),
            v((4, 2, 80, HALF), BF16), v((4, 2, 80, HALF), BF16),
            v((4, 160, HID), BF16),
            v((4, 2, 80, HALF), F32),
            v((4, 2, 80, HALF), BF16), v((4, 2, 80, HALF), BF16),
            v((6, 80, HALF), BF16), v((6, 80, HALF), BF16),
            v((80, HALF), BF16), v((80, HALF), BF16),
            v((N_REQ, TOK, HALF), BF16), v((N_REQ, TOK, HALF), BF16),
            v((TOK, HALF), F32), v((TOK, HALF), F32),
            dma((3,)), dma((8,)), dma((8,)), dma((2,)), dma((2,)), dma((6,)), dma((6,)),
            dma((8,)), dma((8,)), dma((4,)), dma((4,)), dma((6,)), dma((6,)),
            dma((8,)), dma((8,)), dma, dma,
        ],
        name="apply_experts",
        compiler_params=pltpu.CompilerParams(
            collective_id=2, has_side_effects=True, vmem_limit_bytes=60 << 20
        ),
    )(packed, gates, resid, pick, spread, wg, wu, wd)


def tables():
    steps = np.arange(HD // 2, dtype=np.float32) / np.float32(HD // 2)
    freq = (np.float64(ROPE_BASE) ** -steps.astype(np.float64)).astype(np.float32)
    angles = (PUSE * (PLEN + GAP) + np.arange(QTOK)).astype(np.float32)[:, None] * freq[None, :]
    cosine, sine = np.cos(angles.astype(np.float64)), np.sin(angles.astype(np.float64))
    qcos = np.concatenate([cosine, cosine], axis=1).astype(np.float32)
    qsin = np.concatenate([-sine, sine], axis=1).astype(np.float32)
    pick = np.zeros((80, 128), np.float32)
    for r in range(N_REQ):
        for s in range(2 * C):
            pick[r * 2 * C + s, r * TOK + s] = 1
    return freq, qcos, qsin, pick


def per_device(
    hidden_in, queries, question_kv, passage_kv, use_lists, offsets, out_weight, norm_gain,
    router, routes, w_gate, w_up, w_down,
):
    request = lax.axis_index("req")
    core = lax.axis_index("exp") % 2
    freq, qcos, qsin, pick = tables()
    here = use_lists // PASS_DEV == request
    sel = jnp.sum(jnp.where(here, use_lists % PASS_DEV, 0), axis=1).astype(jnp.int32)
    my_uses = lax.dynamic_index_in_dim(use_lists, request, 0, keepdims=False)
    own = my_uses // PASS_DEV
    my_offsets = lax.dynamic_index_in_dim(offsets, request, 0, keepdims=False)
    p_angles = my_offsets.astype(F32)[:, None] * jnp.asarray(freq)[None, :]
    cosine, sine = jnp.cos(p_angles), jnp.sin(p_angles)
    pcos = jnp.concatenate([cosine, cosine], axis=1)
    psin = jnp.concatenate([-sine, sine], axis=1)

    expert_ids = jnp.arange(E, dtype=jnp.int32)
    flat = routes.reshape(-1)
    one_hot = (flat[:, None] == expert_ids[None, :]).astype(jnp.int32)
    ranks = jnp.sum((jnp.cumsum(one_hot, axis=0) - one_hot) * one_hot, axis=-1)
    slots = (flat * TOK + core * C + ranks).reshape(TOK, 2)
    match = slots[:, :, None] == jnp.arange(E * TOK, dtype=jnp.int32)[None, None, :]
    first, second = match[:, 0].astype(F32), match[:, 1].astype(F32)
    spots = (first + second).astype(BF16)
    named = (routes[:, :, None] == expert_ids[None, None, :]).astype(F32)
    diff = named[:, 0] - named[:, 1]

    attended = attention(
        passage_kv, queries, question_kv, sel, own, pcos, psin, jnp.asarray(qcos), jnp.asarray(qsin)
    )
    resid, packed, gates = project(
        attended.reshape(8, 2, TOK, HEADS * HD), out_weight, hidden_in, norm_gain.reshape(1, D),
        router, spots, diff, first, second,
    )
    return experts(
        packed, gates, resid, jnp.asarray(pick, BF16), jnp.asarray(pick.T, BF16),
        w_gate[0], w_up[0], w_down[0],
    )


def solution(mesh):
    in_specs = (
        P(("req", "exp"), None),
        P("req", "exp"),
        P("req", None),
        P("req", "exp", None),
        P(),
        P(),
        P("exp", "req"),
        P(),
        P(),
        P(("req", "exp"), None),
        P("req", None, "exp"),
        P("req", None, "exp"),
        P("req", "exp", None),
    )
    return jax.shard_map(
        per_device, mesh=mesh, in_specs=in_specs, out_specs=P(("req", "exp"), None), check_vma=False
    )
```

time: 673 us -> 264 us (0.39)
  waiting for transfers between devices: 447 us -> 0 us
  Pallas kernels: 0 us -> 242 us
  local copies, waits for them, and re-layouts: 85.8 us -> 15.8 us
  matrix products: 65.9 us -> 0 us
  starting transfers between devices: 19.2 us -> 0 us
  other arithmetic: 21.3 us -> 4.22 us
  blocking collectives: 14.4 us -> 0 us
  between operations: 13.9 us -> 0.09 us
    pallas_call x0 -> x3, Pallas kernels: none -> 242 us  [the longest x1 118 us: experts(): pl.pallas_call(expert_kernel, out_shape=jax.ShapeDtypeStruct((TOK, D), BF...]
    all_to_all x3 -> x0, waiting for transfers between devices: 199 us -> none  [the longest x1 137 us: per_device(): lax.all_to_all(by_head, 'exp', split_axis=2, concat_axis=1, tiled=True)]
    unnamed x5 -> x0, waiting for transfers between devices: 92.6 us -> none
    reduce_scatter x1 -> x0, waiting for transfers between devices: 83.2 us -> none  [per_device(): lax.psum_scatter(head_terms, 'exp', scatter_dimension=0, tiled=True)]
    all_gather x2 -> x0, waiting for transfers between devices: 71.9 us -> none  [the longest x1 71.9 us: per_device(): gathered = lax.all_gather(received, 'exp', axis=0, tiled=True)]
    dot_general x11 -> x0, matrix products: 65.9 us -> none  [the longest x1 12 us: per_device(): jnp.dot(probabilities, all_values, preferred_element_type=jnp.float32)]
    all_to_all x3 -> x0, local copies, waits for them, and re-layouts: 19.9 us -> none  [the longest x1 12.3 us: per_device(): lax.all_to_all(by_head, 'exp', split_axis=2, concat_axis=1, tiled=True)]
    another operation x3 -> x0, local copies, waits for them, and re-layouts: 19.2 us -> none  [the longest x1 14.1 us: per_device(): token_rows = gathered[:, 0].reshape(-1, D)]
  transfers between devices with their start and end apart: 7 -> 0, of which waited for: 6 -> 0; matrix products, arithmetic and copies ran while one was open for 11% -> 0% of each run, Pallas kernels for 0% -> 0%
where the time goes in v1:
time: 264 us; the launch traced here: 262 us
  Pallas kernels  242 us (92%)
  local copies, waits for them, and re-layouts  15.8 us (6%)
  other arithmetic  4.22 us (2%)
    pallas_call x1, Pallas kernels, experts(): pl.pallas_call(expert_kernel, out_shape=jax.ShapeDtypeStruct((TOK, D), BF...  118 us
    pallas_call x1, Pallas kernels, attention(): pl.pallas_call(attention_kernel, out_shape=jax.ShapeDtypeStruct((QTOK, HE...  74.4 us
    pallas_call x1, Pallas kernels, project(): pl.pallas_call(project_kernel, out_shape=(jax.ShapeDtypeStruct((TOK, D),...  50.3 us
    unnamed x25, local copies, waits for them, and re-layouts  14.6 us

profile of v1, /device:TPU:1, one launch (start us, length us, event | category | flops | bytes accessed | tf_op | source)
XLA Modules:
  0.0 262.4 jit_solution(14154456715483946323)
XLA Ops:
  0.0 0.7 fusion.5.sel
  0.7 0.9 convert_reduce_fusion
  1.6 0.9 dynamic-slice_reduce_fusion
  2.5 0.8 fusion.7
  3.2 0.1 pad_maximum_fusion
  3.3 0.7 fusion.1
  4.0 0.1 copy.36.diff
  4.1 0.8 copy.33
  4.8 0.1 eq.53
  4.9 0.1 fusion
  5.0 0.1 reduce_window_sum.11
  5.0 0.2 select_reduce_fusion
  5.2 0.1 reduce_sum.22
  5.3 0.1 copy.34
  5.4 0.7 add_add_fusion
  6.1 0.1 iota_compare_fusion
  6.2 0.0 copy-start
  6.2 1.6 copy-done
  7.8 0.0 copy-start.1
  7.8 1.2 copy-done.1
  9.0 0.0 copy-start.5
  9.0 0.9 copy-done.5
  9.9 0.0 copy-start.7
  9.9 0.9 copy-done.7
  10.8 0.0 copy-start.8
  10.8 0.9 copy-done.8
  11.7 74.4 %attend_passages.1 = bf16[256,384]{1,0:T(8,128)(2,1)S(1)} custom-call(bf16[4,128,2048]{2,1,0:T(8,128)(2,1)S(1)} %copy-done, bf16[256,384]{1,0:T(8,128)(2,1)S(1)} %copy-done.5, bf16[256,2048]{1,0:T(8,128)(2,1)S(1)} %copy-done.1, s32[8]{0:T(128)S(1)} %fusion.5.sel, s32[4]{0:T(128)S(1)} %and_select_fusion.own, f32[4,128]{1,0:T(4,128)S(1)} %get-tuple-element.16.pcos, ...), custom_call_target="tpu_custom_call" | custom-call | tf_op jit(solution)/shard_map/attend_passages/pallas_call | solution.py:204
  86.1 1.8 copy.35.router
  87.9 0.0 copy-start.3
  87.9 1.1 copy-done.3
  89.0 0.0 copy-start.6
  89.0 0.9 copy-done.6
  89.9 0.0 copy-start.9
  89.9 0.7 copy-done.9
  90.6 50.3 %project_heads.1 = (f32[16,6144]{1,0:T(8,128)S(1)}, bf16[8,16,3072]{2,1,0:T(8,128)(2,1)S(1)}, f32[2,16,128]{2,1,0:T(8,128)S(1)}) custom-call(bf16[8,2,16,384]{3,2,1,0:T(8,128)(2,1)S(1)} %bitcast.15, bf16[384,768]{1,0:T(8,128)(2,1)S(1)} %copy-done.3, bf16[16,6144]{1,0:T(8,128)(2,1)S(1)} %copy-done.6, f32[1,6144]{1,0:T(1,128)S(1)} %bitcast.16, ...), custom_call_target="tpu_custom_call" | custom-call | tf_op jit(solution)/shard_map/project_heads/pallas_call | solution.py:344
  141.0 0.0 copy-start.2
  141.0 0.9 copy-done.2
  141.8 0.0 copy-start.4
  141.8 0.7 copy-done.4
  142.6 0.0 copy-start.10
  142.6 0.6 copy-done.10
  143.2 117.6 %apply_experts.1 = bf16[16,6144]{1,0:T(8,128)(2,1)} custom-call(bf16[8,16,3072]{2,1,0:T(8,128)(2,1)} %copy-done.2, f32[2,16,128]{2,1,0:T(8,128)} %copy-done.10, f32[16,6144]{1,0:T(8,128)} %copy-done.4, bf16[80,128]{1,0:T(8,128)(2,1)} %constant.85.clone.pick, bf16[128,80]{1,0:T(8,128)(2,1)} %constant.86.clone.spread, bf16[6144,512]{1,0:T(8,128)(2,1)} %bitcast.17, ...), custom_call_target="tpu_custom_call" | custom-call | tf_op jit(solution)/shard_map/apply_experts/pallas_call | solution.py:555
  260.8 1.6 copy.38
  (4 shorter events, 0.0 us)
Async XLA Ops:
  6.2 1.6 copy-start
  7.8 1.2 copy-start.1
  9.0 0.9 copy-start.5
  9.9 0.9 copy-start.7
  10.8 0.9 copy-start.8
  87.9 1.1 copy-start.3
  89.0 0.9 copy-start.6
  89.9 0.7 copy-start.9
  141.0 0.9 copy-start.2
  141.8 0.7 copy-start.4
  142.6 0.6 copy-start.10
